TPU v7x, 128 devices: a whole 4x4x4 slice. The times are simulated.
128 devices in a mesh: dp: 128 (over y, x, z, core).
Axes of the slice: x: 4, y: 4, z: 4, core: 2. Of those that a mesh axis runs over, the one named last changes fastest.
Arguments:
- features: bfloat16 [1024, 784, 192], P('dp'), may hold values from -21 to 21
- batchnorm_scale: float32 [192], replicated, may hold values from 0.1 to 1.9
- batchnorm_bias: float32 [192], replicated, may hold values from -3 to 3
- w_short: bfloat16 [192, 384], replicated, may hold values from -0.4375 to 0.4375
- ln1_gain: float32 [192], replicated, may hold values from 0.1 to 1.9
- ln1_bias: float32 [192], replicated, may hold values from -3 to 3
- w_qkv: bfloat16 [192, 1152], replicated, may hold values from -0.4375 to 0.4375
- rel_table: float32 [12, 729], replicated, may hold values from -4 to 4
- w_out: bfloat16 [384, 384], replicated, may hold values from -0.875 to 0.875
- ln2_gain: float32 [384], replicated, may hold values from 0.1 to 1.9
- ln2_bias: float32 [384], replicated, may hold values from -3 to 3
- w_fc1: bfloat16 [384, 1536], replicated, may hold values from -0.3125 to 0.3125
- fc1_bias: float32 [1536], replicated, may hold values from -3 to 3
- w_fc2: bfloat16 [1536, 384], replicated, may hold values from -0.15625 to 0.15625
- fc2_bias: float32 [384], replicated, may hold values from -3 to 3
- cotangent: bfloat16 [1024, 196, 384], P('dp'), may hold values from -6 to 6
Outputs:
- layer_out: float32 [1024, 196, 384], P('dp')
- grad_features: float32 [1024, 784, 192], P('dp')
- batchnorm_scale_gradient: float32 [192], replicated
- grad_bn_bias: float32 [192], replicated
- grad_w_short: float32 [192, 384], replicated
- grad_ln1_gain: float32 [192], replicated
- grad_ln1_bias: float32 [192], replicated
- grad_w_qkv: float32 [192, 1152], replicated
- grad_rel_table: float32 [12, 729], replicated
- grad_w_out: float32 [384, 384], replicated
- grad_ln2_gain: float32 [384], replicated
- grad_ln2_bias: float32 [384], replicated
- grad_w_fc1: float32 [384, 1536], replicated
- grad_fc1_bias: float32 [1536], replicated
- grad_w_fc2: float32 [1536, 384], replicated
- grad_fc2_bias: float32 [384], replicated
All inputs are finite; a program needn't handle non-finite values.
Results may differ from a plain program's by a relative error of at most 0.012.
The roundings to bfloat16 on the way count: a program that leaves them out, or rounds other values in their place, can miss the bound.
Values sent between devices are 32-bit elements; how exact they have to be, the bound alone decides.
No kernel may reach another device: no remote copies, remote signals or barrier semaphores. Data moves between devices by JAX's collectives and lax.ppermute only.
A program may use at most 192 MiB of HBM per device.

v0:
```python
from functools import partial

import jax
import jax.numpy as jnp
from jax import lax
from jax.sharding import PartitionSpec as P

HEADS = 12
HEAD = 32
SIDE = 14
TOK = 196


EPS = 1e-05
HIGH = lax.Precision.HIGHEST
FLOAT = jnp.float32
HALF = jnp.bfloat16


def layer_norm(values, gain_vec, shift_vec):
    centre = values - jnp.mean(values, axis=-1, keepdims=True)
    spread = jnp.mean(centre * centre, axis=-1, keepdims=True)
    return centre * lax.rsqrt(spread + EPS) * gain_vec + shift_vec


def pooling(values):
    crop_count = values.shape[0]
    grid = values.reshape(crop_count, SIDE, 2, SIDE, 2, values.shape[-1])
    return jax.nn.logsumexp(grid, axis=(2, 4)).reshape(crop_count, TOK, values.shape[-1])


def weight_grad(left, right):
    return jnp.einsum("cti,ctj->ij", left, right, preferred_element_type=FLOAT)


def input_grad(grad_rows, weight):
    return jnp.einsum("ctj,ij->cti", grad_rows, weight, preferred_element_type=FLOAT)


def offset_tables():
    rel_side = 2 * SIDE - 1
    coord = jnp.arange(SIDE, dtype=jnp.int32)
    offset = coord[:, None] - coord[None, :] + SIDE - 1
    return (offset[:, :, None] == jnp.arange(rel_side, dtype=jnp.int32)[None, None, :]).astype(
        FLOAT
    )


def on_device(
    features,
    batchnorm_scale,
    batchnorm_bias,
    w_short,
    ln1_gain,
    ln1_bias,
    w_qkv,
    rel_table,
    w_out,
    ln2_gain,
    ln2_bias,
    w_fc1,
    fc1_bias,
    w_fc2,
    fc2_bias,
    cotangent,
):
    crop_count = features.shape[0]
    width_out = w_out.shape[1]
    rel_side = 2 * SIDE - 1
    head_scale = HEAD ** (-0.5)
    total_row_count = float(features.shape[0] * features.shape[1] * lax.axis_size("dp"))
    values_in = features.astype(FLOAT)
    sum_rows = lax.psum(jnp.sum(values_in, axis=(0, 1)), "dp")
    bn_centre = sum_rows / total_row_count
    centered_input = values_in - bn_centre
    bn_var = lax.psum(jnp.sum(centered_input * centered_input, axis=(0, 1)), "dp") / total_row_count
    batchnorm_inverse_deviation = lax.rsqrt(bn_var + EPS)
    standardized_input = centered_input * batchnorm_inverse_deviation
    normalized_output = standardized_input * batchnorm_scale + batchnorm_bias
    pooled, pool_back = jax.vjp(pooling, normalized_output)
    pooled_lo = pooled.astype(HALF)
    short = jnp.dot(pooled_lo, w_short, preferred_element_type=FLOAT)
    first_norm, ln1_back = jax.vjp(layer_norm, pooled, ln1_gain, ln1_bias)
    first_lo = first_norm.astype(HALF)
    packed = jnp.dot(first_lo, w_qkv, preferred_element_type=FLOAT).astype(HALF)
    query = packed[..., :width_out].reshape(crop_count, TOK, HEADS, HEAD)
    key_part = packed[..., width_out : 2 * width_out].reshape(crop_count, TOK, HEADS, HEAD)
    value_part = packed[..., 2 * width_out :].reshape(crop_count, TOK, HEADS, HEAD)
    one_hot = offset_tables()
    table_grid = rel_table.reshape(HEADS, rel_side, rel_side)
    bias = jnp.einsum("hab,ima,jnb->hijmn", table_grid, one_hot, one_hot, precision=HIGH).reshape(
        HEADS, TOK, TOK
    )
    scores = (
        jnp.einsum("cihd,cjhd->chij", query, key_part, preferred_element_type=FLOAT) * head_scale
        + bias[None]
    )
    probs = jnp.exp(scores - jax.nn.logsumexp(scores, axis=-1, keepdims=True))
    probs_lo = probs.astype(HALF)
    mixed = jnp.einsum("chij,cjhd->cihd", probs_lo, value_part, preferred_element_type=FLOAT)
    mixed_lo = mixed.reshape(crop_count, TOK, width_out).astype(HALF)
    resid = short + jnp.dot(mixed_lo, w_out, preferred_element_type=FLOAT)
    second_norm, ln2_back = jax.vjp(layer_norm, resid, ln2_gain, ln2_bias)
    second_lo = second_norm.astype(HALF)
    pre_act = jnp.dot(second_lo, w_fc1, preferred_element_type=FLOAT) + fc1_bias
    hidden, gelu_back = jax.vjp(partial(jax.nn.gelu, approximate=False), pre_act)
    hidden_lo = hidden.astype(HALF)
    layer_out = resid + jnp.dot(hidden_lo, w_fc2, preferred_element_type=FLOAT) + fc2_bias
    out_grad = cotangent.astype(FLOAT)
    grad_fc2_bias = jnp.sum(cotangent.astype(FLOAT), axis=(0, 1))
    grad_w_fc2 = weight_grad(hidden_lo, cotangent)
    hidden_grad = input_grad(cotangent, w_fc2)
    pre_grad = gelu_back(hidden_grad)[0].astype(HALF)
    grad_fc1_bias = jnp.sum(pre_grad.astype(FLOAT), axis=(0, 1))
    grad_w_fc1 = weight_grad(second_lo, pre_grad)
    second_grad = input_grad(pre_grad, w_fc1)
    resid_part, grad_ln2_gain, grad_ln2_bias = ln2_back(second_grad)
    resid_grad = out_grad + resid_part
    resid_lo = resid_grad.astype(HALF)
    grad_w_out = weight_grad(mixed_lo, resid_lo)
    grad_w_short = weight_grad(pooled_lo, resid_lo)
    mixed_grad = input_grad(resid_lo, w_out).astype(HALF).reshape(crop_count, TOK, HEADS, HEAD)
    probs_grad = jnp.einsum("cihd,cjhd->chij", mixed_grad, value_part, preferred_element_type=FLOAT)
    value_grad = jnp.einsum("chij,cihd->cjhd", probs_lo, mixed_grad, preferred_element_type=FLOAT)
    score_grad = (
        probs * (probs_grad - jnp.sum(probs_grad * probs, axis=-1, keepdims=True))
    ).astype(HALF)
    query_grad = (
        jnp.einsum("chij,cjhd->cihd", score_grad, key_part, preferred_element_type=FLOAT)
        * head_scale
    )
    key_grad = (
        jnp.einsum("chij,cihd->cjhd", score_grad, query, preferred_element_type=FLOAT) * head_scale
    )
    bias_grad = jnp.sum(score_grad.astype(FLOAT), axis=0).reshape(HEADS, SIDE, SIDE, SIDE, SIDE)
    grad_rel_table = jnp.einsum(
        "hijmn,ima,jnb->hab", bias_grad, one_hot, one_hot, precision=HIGH
    ).reshape(HEADS, rel_side * rel_side)
    packed_grad = jnp.concatenate(
        [
            query_grad.reshape(crop_count, TOK, width_out),
            key_grad.reshape(crop_count, TOK, width_out),
            value_grad.reshape(crop_count, TOK, width_out),
        ],
        axis=-1,
    ).astype(HALF)
    grad_w_qkv = weight_grad(first_lo, packed_grad)
    first_grad = input_grad(packed_grad, w_qkv)
    pooled_part, grad_ln1_gain, grad_ln1_bias = ln1_back(first_grad)
    pooled_grad = pooled_part + input_grad(resid_lo, w_short)
    normalized_output_gradient = pool_back(pooled_grad)[0]
    batchnorm_scale_gradient, grad_bn_bias = lax.psum(
        (
            jnp.sum(normalized_output_gradient * standardized_input, axis=(0, 1)),
            jnp.sum(normalized_output_gradient, axis=(0, 1)),
        ),
        "dp",
    )
    grad_features = batchnorm_inverse_deviation * (
        normalized_output_gradient * batchnorm_scale
        - batchnorm_scale * grad_bn_bias / total_row_count
        - standardized_input * batchnorm_scale * batchnorm_scale_gradient / total_row_count
    )
    (
        grad_w_short,
        grad_ln1_gain,
        grad_ln1_bias,
        grad_w_qkv,
        grad_rel_table,
        grad_w_out,
        grad_ln2_gain,
        grad_ln2_bias,
        grad_w_fc1,
        grad_fc1_bias,
        grad_w_fc2,
        grad_fc2_bias,
    ) = lax.psum(
        (
            grad_w_short,
            grad_ln1_gain,
            grad_ln1_bias,
            grad_w_qkv,
            grad_rel_table,
            grad_w_out,
            grad_ln2_gain,
            grad_ln2_bias,
            grad_w_fc1,
            grad_fc1_bias,
            grad_w_fc2,
            grad_fc2_bias,
        ),
        "dp",
    )
    return (
        layer_out,
        grad_features,
        batchnorm_scale_gradient,
        grad_bn_bias,
        grad_w_short,
        grad_ln1_gain,
        grad_ln1_bias,
        grad_w_qkv,
        grad_rel_table,
        grad_w_out,
        grad_ln2_gain,
        grad_ln2_bias,
        grad_w_fc1,
        grad_fc1_bias,
        grad_w_fc2,
        grad_fc2_bias,
    )


def solution(mesh):
    in_specs = (
        P("dp", None, None),
        P(),
        P(),
        P(),
        P(),
        P(),
        P(),
        P(),
        P(),
        P(),
        P(),
        P(),
        P(),
        P(),
        P(),
        P("dp", None, None),
    )
    out_specs = (
        P("dp", None, None),
        P("dp", None, None),
        P(),
        P(),
        P(),
        P(),
        P(),
        P(),
        P(),
        P(),
        P(),
        P(),
        P(),
        P(),
        P(),
        P(),
    )
    return jax.shard_map(
        on_device, mesh=mesh, in_specs=in_specs, out_specs=out_specs, check_vma=False
    )
```

profile of v0, /device:TPU:0, one launch (start us, length us, event | category | flops | bytes accessed | tf_op | source)
XLA Modules:
  0.0 583.8 jit_solution(1433859356512201165)
XLA Ops:
  7.3 6.6 %copy.79 = bf16[8,784,192]{2,0,1:T(8,128)(2,1)} copy(bf16[8,784,192]{1,2,0:T(8,128)(2,1)} %param.16) | data formatting | bytes 4816896 | tf_op args[0]
  13.9 2.8 convert_reduce_fusion.2
  16.7 68.2 %psum.112 = f32[192]{0:T(256)S(1)} all-reduce(f32[192]{0:T(256)S(1)} %convert_reduce_fusion.2), channel_id=1, replica_groups=mesh['dp'=128] {'dp'}, use_global_device_ids=true, to_apply=%region_1.0 | all-reduce | flops 192 | bytes 1536 | tf_op jit(solution)/shard_map/psum | solution.py:73
  84.9 2.9 fusion.18
  87.8 62.4 %psum.113 = f32[192]{0:T(256)S(1)} all-reduce(f32[192]{0:T(256)S(1)} %fusion.18), channel_id=1, replica_groups=mesh['dp'=128] {'dp'}, use_global_device_ids=true, to_apply=%region_3.0 | all-reduce | flops 192 | bytes 1536 | tf_op jit(solution)/shard_map/psum | solution.py:76
  150.3 5.7 fusion.13
  155.9 4.0 reduce_max.20
  160.1 4.9 exponential_reduce_fusion.1
  166.3 3.1 multiply_reduce_fusion.4
  169.6 1.8 copy.80
  171.8 2.9 copy.82
  174.8 1.7 fusion.25
  177.6 1.5 convolution_convert_fusion
  179.1 1.8 fusion.67
  180.9 2.5 copy.87
  183.4 2.5 copy.86
  185.9 1.6 copy.85
  188.3 11.2 %convolution_bitcast_fusion = f32[12,14,14,14,14]{4,3,2,0,1:T(8,128)} fusion(f32[14,14,12,27,1]{3,1,4,2,0:T(8,128)S(1)} %convolution_bitcast_fusion.5, s32[14,14]{1,0:T(8,128)S(1)} %subtract_add_fusion), kind=kOutput, calls=%fused_computation.30 | convolution fusion | flops 149366704 | bytes 2098768 | tf_op jit(solution)/shard_map/hab,ima,jnb->hijmn/dot_general | solution.py:91
  199.5 27.4 %copy.118 = f32[12,14,14,14,14]{2,1,4,3,0:T(8,128)} copy(f32[12,14,14,14,14]{4,3,2,0,1:T(8,128)} %convolution_bitcast_fusion) | data formatting | bytes 3687936 | tf_op jit(solution)/shard_map/add | solution.py:95
  226.9 12.6 %reshape.233 = f32[12,196,196]{1,2,0:T(8,128)} reshape(f32[12,14,14,14,14]{2,1,4,3,0:T(8,128)} %copy.118) | data formatting | bytes 3687936 | tf_op jit(solution)/shard_map/add | solution.py:95
  239.5 6.0 %fusion = (f32[8,12,196]{2,1,0:T(8,128)S(1)}, f32[8,12,196,196]{2,3,1,0:T(8,128)S(1)}) fusion(f32[12,196,196]{1,2,0:T(8,128)} %reshape.233, bf16[8,196,12,32]{1,3,2,0:T(8,128)(2,1)} %bitcast.149, bf16[8,196,12,32]{1,3,2,0:T(8,128)(2,1)} %bitcast.143), kind=kOutput, calls=%fused_computation.6 | convolution fusion | flops 247072896 | bytes 19079424 | tf_op jit(solution)/shard_map/cihd,cjhd->chij/dot_general | solution.py:95
  246.2 8.4 %exponential_reduce_fusion = f32[8,12,196]{2,1,0:T(8,128)S(1)} fusion(f32[8,12,196,196]{2,3,1,0:T(8,128)S(1)} %get-tuple-element.102, f32[8,12,196]{2,1,0:T(8,128)S(1)} %is-finite_select_fusion.2, f32[12,196,196]{1,2,0:T(8,128)} %reshape.233), kind=kLoop, calls=%fused_computation.4 | loop fusion | flops 14732928 | bytes 16746240 | tf_op jit(solution)/shard_map/reduce_sum | solution.py:98
  255.6 12.2 %convolution_convert_fusion.2 = bf16[8,12,32,196]{3,2,1,0:T(8,128)(2,1)S(1)} fusion(bf16[8,196,12,32]{1,3,2,0:T(8,128)(2,1)} %bitcast.145, f32[8,12,196,196]{2,3,1,0:T(8,128)} %copy-done.2, f32[8,12,196]{2,1,0:T(8,128)S(1)} %log_add_fusion, f32[12,196,196]{1,2,0:T(8,128)} %reshape.233), kind=kOutput, calls=%fused_computation.72 | convolution fusion | flops 251381760 | bytes 19079424 | tf_op jit(solution)/shard_map/chij,cjhd->cihd/dot_general | solution.py:100
  270.8 5.3 fusion.24
  276.1 23.9 %multiply_convert_fusion.1 = (bf16[8,196,1536]{2,1,0:T(8,128)(2,1)}, f32[8,196,1536]{2,1,0:T(8,128)}) fusion(f32[8,196,1536]{2,1,0:T(8,128)S(1)} %get-tuple-element.105, f32[1536]{0:T(1024)S(1)} %copy-done.51, u8[196,1536]{1,0:T(8,128)(4,1)S(1)} %get-tuple-element.65, u8[196,1536]{1,0:T(8,128)(4,1)S(1)} %get-tuple-element.64), kind=kLoop, calls=%fused_computation.17 | loop fusion | flops 170999808 | bytes 24692736 | tf_op jit(solution)/shard_map/convert_element_type | solution.py:107
  300.0 9.2 %convert_reduce_fusion.1 = (f32[1536]{0:T(1024)S(1)}, bf16[8,196,1536]{2,1,0:T(8,128)(2,1)S(1)}) fusion(f32[8,196,1536]{2,1,0:T(8,128)} %get-tuple-element.93, bf16[1536,384]{1,0:T(8,128)(2,1)} %param.29, bf16[8,196,384]{2,0,1:T(8,128)(2,1)} %param.31, f32[8,196,1536]{2,1,0:T(8,128)S(1)} %get-tuple-element.105, f32[1536]{0:T(1024)S(1)} %copy-done.51), kind=kOutput, calls=%fused_computation.15 | convolution fusion | flops 1890630144 | bytes 26480640 | tf_op jit(solution)/shard_map/ctj,ij->cti/dot_general | solution.py:37
  309.2 4.0 convolution_bitcast_fusion.2
  313.2 3.3 fusion.64
  316.4 1.3 multiply_reduce_fusion.1
  317.8 1.6 convert_reduce_fusion.3
  319.5 1.7 convolution_bitcast_fusion.6
  321.2 1.3 convolution_bitcast_fusion.7
  322.5 2.1 convolution_convert_fusion.3
  324.6 1.6 copy.94
  327.4 11.6 %convolution_convert_fusion.1 = bf16[8,12,32,196]{3,2,1,0:T(8,128)(2,1)} fusion(bf16[8,196,12,32]{1,3,2,0:T(8,128)(2,1)S(1)} %bitcast.147, f32[8,12,196,196]{2,3,1,0:T(8,128)} %copy-done.2, f32[8,12,196]{2,1,0:T(8,128)S(1)} %log_add_fusion, f32[12,196,196]{1,2,0:T(8,128)} %reshape.233), kind=kOutput, calls=%fused_computation.71 | convolution fusion | flops 251381760 | bytes 19079424 | tf_op jit(solution)/shard_map/chij,cihd->cjhd/dot_general | solution.py:124
  338.9 18.3 %multiply_reduce_fusion = (f32[8,12,196]{2,1,0:T(8,128)S(1)}, f32[8,12,196,196]{2,3,1,0:T(8,128)}) fusion(f32[8,12,196,196]{2,3,1,0:T(8,128)} %copy-done.2, f32[8,12,196]{2,1,0:T(8,128)S(1)} %log_add_fusion, f32[12,196,196]{1,2,0:T(8,128)} %reshape.233, bf16[8,196,12,32]{1,3,2,0:T(8,128)(2,1)} %bitcast.148, bf16[8,196,12,32]{1,3,2,0:T(8,128)(2,1)} %bitcast.146), kind=kOutput, calls=%fused_computation.2 | convolution fusion | flops 254448768 | bytes 33906432 | tf_op jit(solution)/shard_map/cihd,cjhd->chij/dot_general | solution.py:123
  357.3 17.2 %convert_reduce_fusion = (f32[12,196,196]{1,2,0:T(8,128)}, bf16[8,12,196,196]{2,3,1,0:T(8,128)(2,1)S(1)}) fusion(f32[8,12,196,196]{2,3,1,0:T(8,128)} %get-tuple-element.108, f32[8,12,196]{2,1,0:T(8,128)S(1)} %get-tuple-element.107, f32[8,12,196]{2,1,0:T(8,128)S(1)} %log_add_fusion, f32[12,196,196]{1,2,0:T(8,128)S(1)} %copy-done.3, f32[8,12,196,196]{2,3,1,0:T(8,128)} %copy-done.2), kind=kLoop, calls=%fused_computation | loop fusion | flops 29042496 | bytes 40717824 | tf_op jit(solution)/shard_map/reduce_sum | solution.py:135
  374.5 5.8 multiply_convert_fusion.2
  380.4 3.0 multiply_convert_fusion.3
  383.4 6.9 %convolution_bitcast_fusion.1 = f32[1536,384]{1,0:T(8,128)} fusion(bf16[8,196,1536]{2,1,0:T(8,128)(2,1)} %get-tuple-element.92, bf16[8,196,384]{2,0,1:T(8,128)(2,1)S(1)} %copy-done.25), kind=kOutput, calls=%fused_computation.58 | convolution fusion | flops 1849688064 | bytes 8380416 | tf_op jit(solution)/shard_map/cti,ctj->ij/dot_general | solution.py:33
  390.3 1.5 copy.100
  391.8 2.7 copy.98
  394.5 2.7 copy.99
  397.3 4.2 convolution_bitcast_fusion.3
  402.7 6.0 %add_add_fusion.1 = f32[8,196,384]{2,1,0:T(8,128)S(1)} fusion(f32[8,196,384]{2,1,0:T(8,128)} %copy-done.5, bf16[8,196,1536]{2,1,0:T(8,128)(2,1)} %get-tuple-element.92, f32[384]{0:T(512)S(1)} %copy-done.58, bf16[1536,384]{1,0:T(8,128)(2,1)S(1)} %copy-done.57), kind=kOutput, calls=%fused_computation.64 | convolution fusion | flops 1850892288 | bytes 10814976 | tf_op jit(solution)/shard_map/dot_general | solution.py:108
  408.8 1.9 copy.105
  411.7 1.6 fusion.65
  413.3 1.3 multiply_reduce_fusion.5
  414.6 2.0 add_add_fusion.3
  416.6 2.8 copy.101
  419.5 2.6 negate_add_fusion
  423.1 2.9 fusion.21
  426.0 12.8 %reshape.214 = f32[12,14,14,14,14]{2,1,4,3,0:T(8,128)} reshape(f32[12,196,196]{1,2,0:T(8,128)} %get-tuple-element.90) | data formatting | bytes 3687936 | tf_op jit(solution)/shard_map/reshape | solution.py:135
  438.8 29.6 %copy.102 = f32[12,14,14,14,14]{3,4,1,2,0:T(8,128)} copy(f32[12,14,14,14,14]{2,1,4,3,0:T(8,128)} %reshape.214) | data formatting | bytes 3687936 | tf_op jit(solution)/shard_map/reshape | solution.py:135
  468.4 16.8 %convolution_bitcast_fusion.4 = f32[27,12,14,14]{0,3,2,1:T(8,128)S(1)} fusion(f32[12,14,14,14,14]{3,4,1,2,0:T(8,128)} %copy.102, s32[14,14]{1,0:T(8,128)S(1)} %copy-done.32), kind=kOutput, calls=%fused_computation.83 | convolution fusion | flops 149366704 | bytes 2098768 | tf_op jit(solution)/shard_map/hijmn,ima,jnb->hab/dot_general | solution.py:136
  485.3 1.3 convolution_bitcast_fusion.8
  486.7 66.4 %all-reduce = (f32[192]{0:T(256)S(1)}, f32[192]{0:T(256)S(1)}, f32[192]{0:T(256)}, f32[192]{0:T(256)}, f32[12,729]{1,0:T(8,128)}, /*index=5*/f32[384]{0:T(512)}, f32[384]{0:T(512)}, f32[1536]{0:T(1024)}, f32[384]{0:T(512)}) all-reduce(f32[192]{0:T(256)S(1)} %get-tuple-element.67, ...), channel_id=1, replica_groups=mesh['dp'=128] {'dp'}, use_global_device_ids=true, to_apply=%region_20.0 | all-reduce | flops 12204 | bytes 97632 | tf_op jit(solution)/shard_map/psum | solution.py:152
  553.1 6.7 %fusion.16 = f32[8,784,192]{2,0,1:T(8,128)} fusion(bf16[8,784,192]{2,0,1:T(8,128)(2,1)} %copy.79, f32[192]{0:T(256)S(1)} %get-tuple-element.114, f32[192]{0:T(256)S(1)} %multiply_multiply_fusion.7, f32[8,14,14,192]{3,0,2,1:T(8,128)} %copy-done.15, f32[8,14,14,192]{3,0,2,1:T(8,128)S(1)} %copy-done.10, f32[192]{0:T(256)S(1)} %copy-done.48, ...), kind=kLoop, calls=%fused_computation.41 | loop fusion | flops 15654912 | bytes 9638400 | tf_op jit(solution)/shard_map/mul | solution.py:159
  559.8 7.1 %copy.106 = f32[8,784,192]{1,2,0:T(8,128)} copy(f32[8,784,192]{2,0,1:T(8,128)} %fusion.16) | data formatting | bytes 9633792
  566.9 1.8 copy.133
  568.7 2.1 copy.134
  570.9 1.9 copy.135
  572.8 1.4 copy.136
  575.3 1.4 copy.137
  (148 shorter events, 14.4 us)
Async XLA Ops:
  7.2 263.5 %copy-start = (bf16[384,1536]{1,0:T(8,128)(2,1)S(1)}, bf16[384,1536]{1,0:T(8,128)(2,1)}, u32[]{:S(2)}) copy-start(bf16[384,1536]{1,0:T(8,128)(2,1)} %param.27) | copy-start | bytes 3538948
  7.2 559.7 %all-reduce.4.cloned.1.call-start = ((), (), s32[]{:S(2)}) async-start(), calls=%async_computation | async-start | bytes 12976128 | tf_op jit(solution)/shard_map/psum | solution.py:177
  7.3 181.0 %copy-start.31 = (s32[14,14]{1,0:T(8,128)}, s32[14,14]{1,0:T(8,128)S(1)}, u32[]{:S(2)}) copy-start(s32[14,14]{1,0:T(8,128)S(1)} %subtract_add_fusion) | copy-start | bytes 2356
  13.9 136.3 %copy-start.43 = (f32[192]{0:T(256)S(1)}, f32[192]{0:T(256)}, u32[]{:S(2)}) copy-start(f32[192]{0:T(256)} %param.17) | copy-start | bytes 2308
  13.9 136.3 %copy-start.47 = (f32[192]{0:T(256)S(1)}, f32[192]{0:T(256)}, u32[]{:S(2)}) copy-start(f32[192]{0:T(256)} %param.18) | copy-start | bytes 2308
  84.9 71.1 %copy-start.41 = (f32[192]{0:T(256)}, f32[192]{0:T(256)S(1)}, u32[]{:S(2)}) copy-start(f32[192]{0:T(256)S(1)} %broadcast_multiply_fusion.2) | copy-start | bytes 2308
  150.3 5.7 copy-start.45
  160.1 4.9 copy-start.9
  165.0 1.2 copy-start.11
  166.3 3.1 copy-start.39
  171.4 3.3 copy-start.18
  171.5 4.9 copy-start.33
  171.8 4.7 copy-start.37
  174.7 2.9 copy-start.29
  174.7 2.9 copy-start.49
  174.7 2.9 copy-start.55
  174.7 1.7 copy-start.35
  176.5 1.2 copy-start.6
  245.5 0.7 copy-start.26
  245.5 9.1 %copy-start.2 = (f32[8,12,196,196]{2,3,1,0:T(8,128)}, f32[8,12,196,196]{2,3,1,0:T(8,128)S(1)}, u32[]{:S(2)}) copy-start(f32[8,12,196,196]{2,3,1,0:T(8,128)S(1)} %get-tuple-element.102) | copy-start | bytes 44255236
  255.6 12.2 %copy-start.27 = (bf16[384,384]{1,0:T(8,128)(2,1)S(1)}, bf16[384,384]{1,0:T(8,128)(2,1)}, u32[]{:S(2)}) copy-start(bf16[384,384]{1,0:T(8,128)(2,1)} %param.24) | copy-start | bytes 884740
  267.8 1.4 copy-start.7
  267.8 1.4 copy-start.28
  270.0 47.8 %copy-start.5 = (f32[8,196,384]{2,1,0:T(8,128)}, f32[8,196,384]{2,1,0:T(8,128)S(1)}, u32[]{:S(2)}) copy-start(f32[8,196,384]{2,1,0:T(8,128)S(1)} %get-tuple-element.104) | copy-start | bytes 7225348
  270.0 0.7 copy-start.40
  270.0 0.8 copy-start.51
  270.0 0.8 copy-start.52
  316.4 1.4 copy-start.24
  319.5 3.1 copy-start.12
  326.2 1.1 copy-start.16
  338.9 18.3 %copy-start.3 = (f32[12,196,196]{1,2,0:T(8,128)S(1)}, f32[12,196,196]{1,2,0:T(8,128)}, u32[]{:S(2)}) copy-start(f32[12,196,196]{1,2,0:T(8,128)} %reshape.233) | copy-start | bytes 5531908
  374.5 5.8 %copy-start.14 = (bf16[8,196,384]{1,2,0:T(8,128)(2,1)S(1)}, bf16[8,196,384]{1,2,0:T(8,128)(2,1)}, u32[]{:S(2)}) copy-start(bf16[8,196,384]{1,2,0:T(8,128)(2,1)} %copy.87) | copy-start | bytes 3612676
  380.4 3.0 copy-start.25
  383.4 6.9 %copy-start.17 = (bf16[8,12,32,196]{3,2,1,0:T(8,128)(2,1)S(1)}, bf16[8,12,32,196]{3,2,1,0:T(8,128)(2,1)}, u32[]{:S(2)}) copy-start(bf16[8,12,32,196]{3,2,1,0:T(8,128)(2,1)} %convolution_convert_fusion.1) | copy-start | bytes 3612676
  391.8 5.4 copy-start.8
  391.8 5.4 copy-start.34
  391.8 5.4 copy-start.36
  391.8 5.4 copy-start.50
  391.8 5.4 copy-start.56
  401.5 1.3 copy-start.57
  401.5 1.3 copy-start.58
  408.7 1.9 copy-start.21
  408.7 2.3 copy-start.22
  408.7 2.9 copy-start.23
  408.8 3.0 copy-start.30
  411.7 1.6 copy-start.38
  413.3 1.3 copy-start.13
  416.6 5.4 copy-start.44
  416.6 5.4 copy-start.46
  416.6 5.4 copy-start.48
  419.4 3.1 copy-start.4
  419.4 3.6 copy-start.10
  419.4 3.6 copy-start.42
  423.1 3.0 copy-start.15
  438.8 29.6 %copy-start.32 = (s32[14,14]{1,0:T(8,128)S(1)}, s32[14,14]{1,0:T(8,128)}, u32[]{:S(2)}) copy-start(s32[14,14]{1,0:T(8,128)} %copy-done.31) | copy-start | bytes 2356
  553.1 6.7 %copy-start.53 = (f32[192]{0:T(256)}, f32[192]{0:T(256)S(1)}, u32[]{:S(2)}) copy-start(f32[192]{0:T(256)S(1)} %get-tuple-element.114) | copy-start | bytes 2308
  553.1 6.7 %copy-start.54 = (f32[192]{0:T(256)}, f32[192]{0:T(256)S(1)}, u32[]{:S(2)}) copy-start(f32[192]{0:T(256)S(1)} %get-tuple-element.115) | copy-start | bytes 2308
  566.9 5.9 %copy-start.20 = (f32[384,1536]{1,0:T(8,128)S(1)}, f32[384,1536]{1,0:T(8,128)}, u32[]{:S(2)}) copy-start(f32[384,1536]{1,0:T(8,128)} %get-tuple-element.124) | copy-start | bytes 7077892
  572.8 2.5 copy-start.19
  572.8 3.9 copy-start.1
Sparse Core Ops, SparseCore 0:
  401.6 157.1 all-reduce.3
where the time goes:
time: 589 us; the launch traced here: 584 us
  blocking collectives  197 us (33%)
  local copies, waits for them, and re-layouts  141 us (24%)
  matrix products  138 us (23%)
  other arithmetic  93.3 us (16%)
  between operations  15 us (3%)
    psum x1, blocking collectives, on_device(): sum_rows = lax.psum(jnp.sum(values_in, axis=(0, 1)), 'dp')  68.2 us
    psum x1, blocking collectives, on_device(): lax.psum((jnp.sum(normalized_output_gradient * standardized_input, axis=(...  66.4 us
    psum x1, blocking collectives, on_device(): lax.psum(jnp.sum(centered_input * centered_input, axis=(0, 1)), 'dp')  62.4 us
    reshape x2, local copies, waits for them, and re-layouts, on_device(): jnp.sum(score_grad.astype(FLOAT), axis=0)  42.4 us
    add x2, local copies, waits for them, and re-layouts, on_device(): jnp.einsum('cihd,cjhd->chij', query, key_part, preferred_element_type=FLOAT)  40 us
    unnamed x126, local copies, waits for them, and re-layouts  33 us
    convert_element_type x1, other arithmetic, on_device(): hidden_lo = hidden.astype(HALF)  23.9 us
    dot_general x1, matrix products, on_device(): jnp.einsum('cihd,cjhd->chij', mixed_grad, value_part, preferred_element_t...  18.3 us
  transfers between devices with their start and end apart: 1, of which 0 were waited for; matrix products, arithmetic and copies ran while one was open for 16% of the time, Pallas kernels for 0%

commit v1 on v0

v1 whole, which is shorter than its diff:
```python
import jax
import jax.numpy as jnp
import numpy as np
from jax import lax
from jax.experimental import pallas as pl
from jax.experimental.pallas import tpu as pltpu
from jax.sharding import PartitionSpec as P

HEADS = 12
HEAD = 32
SIDE = 14
TOK = 196
TP = 208
GRID2 = 2 * SIDE
CELLS = 784
D_IN = 192
D = 384
FF = 1536
CROPS = 8
ROWS = TOK * CROPS
ROWS_P = TP * CROPS
REL = 27
TAB = 768
SPREAD = 384

EPS = 1e-05
FLOAT = jnp.float32
HALF = jnp.bfloat16
LOG2E = 1.4426950408889634
SCALE = HEAD ** (-0.5)
NN = (((1,), (0,)), ((), ()))
NT = (((1,), (1,)), ((), ()))
TN = (((0,), (0,)), ((), ()))
VMEM_LIMIT = 56 * 1024 * 1024


def dot(left, right, dims=NN):
    return lax.dot_general(left, right, dims, preferred_element_type=FLOAT)


def split3(value):
    hi = value.astype(HALF)
    rest = value - hi.astype(FLOAT)
    mid = rest.astype(HALF)
    lo = (rest - mid.astype(FLOAT)).astype(HALF)
    return hi, mid, lo


def params(limit=VMEM_LIMIT):
    return pltpu.CompilerParams(vmem_limit_bytes=limit)


def cost(flops, bytes_accessed, transcendentals=0):
    return pl.CostEstimate(
        flops=int(flops), bytes_accessed=int(bytes_accessed), transcendentals=int(transcendentals)
    )


def whole(shape):
    return pl.BlockSpec(shape, lambda *_: (0,) * len(shape))


def select_matrix():
    table = np.zeros((4 * TP, CELLS), np.float32)
    for part in range(4):
        a, b = divmod(part, 2)
        for t in range(TOK):
            i, j = divmod(t, SIDE)
            table[part * TP + t, (2 * i + a) * GRID2 + 2 * j + b] = 1.0
    return table


def spread_matrix():
    table = np.zeros((SPREAD, TP), np.float32)
    for t in range(TOK):
        i, j = divmod(t, SIDE)
        table[REL * i + j, t] = 1.0
    return table


def reverse_spread_matrix():
    table = np.zeros((TP, SPREAD), np.float32)
    for t in range(TOK):
        i, j = divmod(t, SIDE)
        table[t, 364 - (REL * i + j)] = 1.0
    return table


def stats_kernel(x_ref, out_ref):
    pieces = []
    step = 32
    for block in range(D_IN // step):
        rows = slice(block * step, (block + 1) * step)
        total = x_ref[0, rows, :].astype(FLOAT)
        for crop in range(1, CROPS):
            total = total + x_ref[crop, rows, :].astype(FLOAT)
        total = jnp.sum(total, axis=1, keepdims=True)
        mean = total * (1.0 / (CROPS * CELLS))
        square = jnp.zeros((step, CELLS), FLOAT)
        for crop in range(CROPS):
            centre = x_ref[crop, rows, :].astype(FLOAT) - mean
            square = square + centre * centre
        square = jnp.sum(square, axis=1, keepdims=True)
        lane = lax.broadcasted_iota(jnp.int32, (step, 128), 1)
        pieces.append(jnp.where(lane == 0, mean, jnp.where(lane == 1, square, 0.0)))
    turned = jnp.concatenate(pieces, axis=0).T
    pad = jnp.zeros((1, 64), FLOAT)
    row = jnp.concatenate([turned[0:1], pad, turned[1:2], pad], axis=1)
    out_ref[...] = jnp.broadcast_to(row[None], out_ref.shape)


def local_stats(cells, copies):
    return pl.pallas_call(
        stats_kernel,
        out_shape=jax.ShapeDtypeStruct((copies, 1, 512), FLOAT),
        compiler_params=params(),
        name="stats",
        cost_estimate=cost(8e6, 2.8e6),
    )(cells)


def batch_coefficients(gathered):
    count = gathered.shape[0]
    means = gathered[:, 0, 0:D_IN]
    squares = gathered[:, 0, 256 : 256 + D_IN]
    mean = jnp.sum(means, axis=0, keepdims=True) * (1.0 / count)
    off = means - mean
    local = float(CROPS * CELLS)
    var = jnp.sum(squares, axis=0, keepdims=True) + local * jnp.sum(
        off * off, axis=0, keepdims=True
    )
    return mean, lax.rsqrt(var * (1.0 / (local * count)) + EPS)


def select_kernel(s_ref, x_ref, out_ref):
    out_ref[0] = dot(s_ref[...], x_ref[0], NT).astype(HALF)


def select_cells(picks, cells):
    return pl.pallas_call(
        select_kernel,
        grid=(CROPS,),
        in_specs=[
            whole((4 * TP, CELLS)),
            pl.BlockSpec((1, D_IN, CELLS), lambda c: (c, 0, 0)),
        ],
        out_specs=pl.BlockSpec((1, 4 * TP, D_IN), lambda c: (c, 0, 0)),
        out_shape=jax.ShapeDtypeStruct((CROPS, 4 * TP, D_IN), HALF),
        compiler_params=params(),
        name="select_cells",
        cost_estimate=cost(3e9, 7e6),
    )(picks, cells)


def bias_kernel(table_ref, spread_ref, out_ref, rows_ref):
    table = table_ref[0] * LOG2E
    base = pltpu.roll(jnp.broadcast_to(table, (16, TAB)), 0, 1, stride=1, stride_axis=0)
    for r in range(SIDE):
        rolled = pltpu.roll(base, (TAB - 364 + REL * r) % TAB, 1)
        rows_ref[SIDE * r : SIDE * (r + 1), :] = rolled[:SIDE, :SPREAD]
    rows_ref[TOK:, :] = jnp.zeros((TP - TOK, SPREAD), FLOAT)
    value = jnp.zeros((TP, TP), FLOAT)
    for part in split3(rows_ref[...]):
        value = value + dot(part, spread_ref[...])
    row = lax.broadcasted_iota(jnp.int32, (TP, TP), 0)
    out_ref[0] = jnp.where(row < TOK, value, -1e30)


def expand_bias(rel_table, spread):
    table = jnp.pad(rel_table, ((0, 0), (0, TAB - REL * REL))).reshape(HEADS, 1, TAB)
    return pl.pallas_call(
        bias_kernel,
        grid=(HEADS,),
        in_specs=[
            pl.BlockSpec((1, 1, TAB), lambda h: (h, 0, 0)),
            whole((SPREAD, TP)),
        ],
        out_specs=pl.BlockSpec((1, TP, TP), lambda h: (h, 0, 0)),
        out_shape=jax.ShapeDtypeStruct((HEADS, TP, TP), FLOAT),
        scratch_shapes=[pltpu.VMEM((TP, SPREAD), FLOAT)],
        compiler_params=params(),
        name="expand_bias",
        cost_estimate=cost(2e9, 3e6),
    )(table, spread)


def table_kernel(d_ref, spread_ref, out_ref, rows_ref):
    value = jnp.zeros((TP, SPREAD), FLOAT)
    for part in split3(d_ref[0]):
        value = value + dot(part, spread_ref[...])
    rows_ref[:, :SPREAD] = value
    rows_ref[:, SPREAD:] = jnp.zeros((TP, TAB - SPREAD), FLOAT)
    total = jnp.zeros((16, TAB), FLOAT)
    for r in range(SIDE):
        total = total + pltpu.roll(rows_ref[SIDE * r : SIDE * r + 16, :], REL * r, 1)
    row = lax.broadcasted_iota(jnp.int32, (16, TAB), 0)
    total = pltpu.roll(jnp.where(row < SIDE, total, 0.0), 0, 1, stride=1, stride_axis=0)
    out_ref[0] = jnp.sum(total, axis=0, keepdims=True)


def reduce_table(grad_bias, spread):
    return pl.pallas_call(
        table_kernel,
        grid=(HEADS,),
        in_specs=[
            pl.BlockSpec((1, TP, TP), lambda h: (h, 0, 0)),
            whole((TP, SPREAD)),
        ],
        out_specs=pl.BlockSpec((1, 1, TAB), lambda h: (h, 0, 0)),
        out_shape=jax.ShapeDtypeStruct((HEADS, 1, TAB), FLOAT),
        scratch_shapes=[pltpu.VMEM((TP, TAB), FLOAT)],
        compiler_params=params(),
        name="reduce_table",
        cost_estimate=cost(2e9, 3e6),
    )(grad_bias, spread)


def normalised(x, coef_mean, coef_inv, scale, bias):
    return (x - coef_mean) * coef_inv * scale + bias


def pool_parts(x_ref, mean, inv, scale, bias):
    parts = [
        normalised(x_ref[0, part * TP : (part + 1) * TP, :].astype(FLOAT), mean, inv, scale, bias)
        for part in range(4)
    ]
    return parts


def norm_rows(value):
    centre = value - jnp.mean(value, axis=-1, keepdims=True)
    inverse = lax.rsqrt(jnp.mean(centre * centre, axis=-1, keepdims=True) + EPS)
    return centre * inverse, inverse


def put_rows(ref, crop, value):
    for group in range(ref.shape[0]):
        piece = value[:, group * 128 : (group + 1) * 128]
        if piece.shape[1] < 128:
            rest = jnp.zeros((piece.shape[0], 128 - piece.shape[1]), piece.dtype)
            piece = jnp.concatenate([piece, rest], axis=1)
        ref[group, pl.ds(crop, TP, stride=CROPS), :] = piece


def take_rows(ref, crop):
    pieces = [ref[group, pl.ds(crop, TP, stride=CROPS), :] for group in range(ref.shape[0])]
    return jnp.concatenate(pieces, axis=1)


def head_masks():
    lane = lax.broadcasted_iota(jnp.int32, (1, 128), 1)
    return [(lane // HEAD == k).astype(HALF) for k in range(4)]


def attention_kernel(
    gathered_ref,
    x_ref,
    bn_scale_ref,
    bn_bias_ref,
    gain_ref,
    shift_ref,
    w_ref,
    bias_ref,
    qkv_ref,
    probs_ref,
    attn_ref,
    pooled_ref,
    coef_ref,
):
    crop = pl.program_id(0)

    @pl.when(crop == 0)
    def _():
        mean, inv = batch_coefficients(gathered_ref[...])
        coef_ref[...] = jnp.zeros_like(coef_ref)
        coef_ref[0:1, :] = mean
        coef_ref[1:2, :] = inv

    mean = coef_ref[0:1, :]
    inv = coef_ref[1:2, :]
    parts = pool_parts(x_ref, mean, inv, bn_scale_ref[...], bn_bias_ref[...])
    top = jnp.maximum(jnp.maximum(parts[0], parts[1]), jnp.maximum(parts[2], parts[3]))
    pooled = top + jnp.log(sum(jnp.exp(part - top) for part in parts))
    put_rows(pooled_ref, crop, pooled)
    z, _ = norm_rows(pooled)
    first = (z * gain_ref[...] + shift_ref[...]).astype(HALF)
    qkv_ref[0] = dot(first, w_ref[...]).astype(HALF)
    value_t = qkv_ref[0, :, 2 * D :].astype(FLOAT).T.astype(HALF)
    masks = head_masks()
    heads = []
    for head in range(HEADS):
        group = head // 4
        lanes = slice(group * 128, (group + 1) * 128)
        query = qkv_ref[0, :, lanes] * masks[head % 4]
        key = qkv_ref[0, :, D + group * 128 : D + (group + 1) * 128]
        scores = dot(key, query, NT) * (SCALE * LOG2E) + bias_ref[head]
        weight = jnp.exp2(scores - jnp.max(scores, axis=0, keepdims=True))
        weight = weight * (1.0 / jnp.sum(weight, axis=0, keepdims=True))
        probs = weight.astype(HALF)
        probs_ref[0, head] = probs
        heads.append(dot(value_t[head * HEAD : (head + 1) * HEAD, :], probs))
    attn = jnp.concatenate(heads, axis=0).T
    put_rows(attn_ref, crop, attn.astype(HALF).astype(FLOAT))


def attention(gathered, picked, bn_scale, bn_bias, gain, shift, w_qkv, bias):
    return pl.pallas_call(
        attention_kernel,
        grid=(CROPS,),
        in_specs=[
            whole(gathered.shape),
            pl.BlockSpec((1, 4 * TP, D_IN), lambda c: (c, 0, 0)),
            whole((1, D_IN)),
            whole((1, D_IN)),
            whole((1, D_IN)),
            whole((1, D_IN)),
            whole((D_IN, 3 * D)),
            whole((HEADS, TP, TP)),
        ],
        out_specs=[
            pl.BlockSpec((1, TP, 3 * D), lambda c: (c, 0, 0)),
            pl.BlockSpec((1, HEADS, TP, TP), lambda c: (c, 0, 0, 0)),
            whole((3, ROWS_P, 128)),
            whole((2, ROWS_P, 128)),
            whole((8, D_IN)),
        ],
        out_shape=[
            jax.ShapeDtypeStruct((CROPS, TP, 3 * D), HALF),
            jax.ShapeDtypeStruct((CROPS, HEADS, TP, TP), HALF),
            jax.ShapeDtypeStruct((3, ROWS_P, 128), FLOAT),
            jax.ShapeDtypeStruct((2, ROWS_P, 128), FLOAT),
            jax.ShapeDtypeStruct((8, D_IN), FLOAT),
        ],
        compiler_params=params(),
        name="attention",
        cost_estimate=cost(4e9, 2.5e7, 4e6),
    )(gathered, picked, bn_scale, bn_bias, gain, shift, w_qkv, bias)


ERFC_P = 0.315
ERFC = (
    0.12566069143336625,
    0.12585512941590216,
    0.11090152008791473,
    0.10280489691671746,
    0.002058691612166641,
    0.12931269519223043,
    -0.13178668519368678,
    0.03519319657675152,
)


def normal_parts(u):
    size = jnp.abs(u)
    bell = jnp.exp2(u * u * (-0.5 * LOG2E))
    t = 1.0 / (1.0 + ERFC_P * size)
    series = jnp.full_like(t, ERFC[-1])
    for factor in ERFC[-2::-1]:
        series = series * t + factor
    tail = series * t * bell
    return jnp.where(u < 0, tail, 1.0 - tail), bell * (1.0 / np.sqrt(2 * np.pi))


HALF_ROWS = 5632
PIECES = 64
LATE_ROWS = 2048
AT_OUT0 = FF // 128 * D
AT_SHORT0 = AT_OUT0 + 2 * D
AT_SUMS = AT_SHORT0 + D_IN
AT_OUT1 = FF // 128 * D
AT_SHORT1 = AT_OUT1 + D

FC_ROWS = 224
FC_STEPS = ROWS // FC_ROWS
FC_COLS = 512


def feed_kernel(
    core_ref,
    attn_ref,
    pooled_ref,
    cot_ref,
    w_short_ref,
    w_out_ref,
    gain_ref,
    shift_ref,
    w1_ref,
    b1_ref,
    w2_ref,
    b2_ref,
    out_ref,
    dattn_ref,
    dshort_ref,
    message_ref,
    sums1_ref,
    sums_ref,
):
    step = pl.program_id(0)
    core = core_ref[0]
    first_half = pl.multiple_of(core * HALF_ROWS, HALF_ROWS)
    second_half = pl.multiple_of((1 - core) * HALF_ROWS, HALF_ROWS)

    def add(base, at, value):
        count = value.shape[0]
        for k in range(value.shape[1] // 128):
            place = pl.ds(pl.multiple_of(base + at + k * count, 8), count)
            message_ref[place, :] += value[:, k * 128 : (k + 1) * 128]

    @pl.when(step == 0)
    def _():
        message_ref[...] = jnp.zeros_like(message_ref)
        sums1_ref[...] = jnp.zeros_like(sums1_ref)
        sums_ref[...] = jnp.zeros_like(sums_ref)
        dattn_ref[:, ROWS:, :] = jnp.zeros((3, ROWS_P - ROWS, 128), FLOAT)
        dshort_ref[:, ROWS:, :] = jnp.zeros((2, ROWS_P - ROWS, 128), FLOAT)

    rows = pl.ds(pl.multiple_of(step * FC_ROWS, FC_ROWS), FC_ROWS)
    attn_wide = jnp.concatenate([attn_ref[k] for k in range(3)], axis=1)
    pooled_wide = jnp.concatenate([pooled_ref[k] for k in range(2)], axis=1)[:, :D_IN]
    attn = attn_wide.astype(HALF)
    pooled = pooled_wide.astype(HALF)
    cot = cot_ref[...]
    y1 = dot(pooled, w_short_ref[...]) + dot(attn, w_out_ref[...])
    z, inverse = norm_rows(y1)
    second = (z * gain_ref[...] + shift_ref[...]).astype(HALF)
    out = y1 + b2_ref[...]
    back = jnp.zeros((FC_ROWS, D), FLOAT)
    second_t = second.astype(FLOAT).T.astype(HALF)
    cot_t = cot.astype(FLOAT).T.astype(HALF)
    for block in range(FF // FC_COLS):
        cols = slice(block * FC_COLS, (block + 1) * FC_COLS)
        u = dot(second, w1_ref[:, cols]) + b1_ref[:, cols]
        cdf, bell = normal_parts(u)
        hidden = (u * cdf).astype(HALF)
        dhidden = dot(cot, w2_ref[cols, :], NT)
        du = (dhidden * (cdf + u * bell)).astype(HALF)
        out = out + dot(hidden, w2_ref[cols, :])
        back = back + dot(du, w1_ref[:, cols], NT)
        at = block * (FC_COLS // 128) * D
        add(first_half, at, dot(second_t, du))
        add(second_half, at, dot(cot_t, hidden))
        sums1_ref[:, cols] += jnp.sum(du.astype(FLOAT), axis=0, keepdims=True)
    out_ref[...] = out
    wide_cot = cot.astype(FLOAT)
    dz = back * gain_ref[...]
    dy1 = wide_cot + inverse * (
        dz
        - jnp.mean(dz, axis=-1, keepdims=True)
        - z * jnp.mean(dz * z, axis=-1, keepdims=True)
    )
    low = dy1.astype(HALF)
    dattn = dot(low, w_out_ref[...], NT).astype(HALF).astype(FLOAT)
    for k in range(3):
        dattn_ref[k, rows, :] = dattn[:, k * 128 : (k + 1) * 128]
    dshort = dot(low, w_short_ref[...], NT)
    dshort_ref[0, rows, :] = dshort[:, :128]
    dshort_ref[1, rows, :] = jnp.concatenate(
        [dshort[:, 128:], jnp.zeros((FC_ROWS, 256 - D_IN), FLOAT)], axis=1
    )
    gout = dot(attn_wide.T.astype(HALF), low)
    add(first_half, AT_OUT0, gout[:, : 2 * 128])
    add(second_half, AT_OUT1, gout[:, 2 * 128 :])
    gshort = dot(pooled_wide.T.astype(HALF), low)
    add(first_half, AT_SHORT0, gshort[:, :128])
    add(second_half, AT_SHORT1, gshort[:, 128:])
    sums_ref[0:1, :] += jnp.sum(back * z, axis=0, keepdims=True)
    sums_ref[1:2, :] += jnp.sum(back, axis=0, keepdims=True)
    sums_ref[2:3, :] += jnp.sum(wide_cot, axis=0, keepdims=True)

    @pl.when(step == FC_STEPS - 1)
    def _():
        pieces = [sums1_ref[:, k * 128 : (k + 1) * 128] for k in range(FF // 128)]
        for line in range(3):
            pieces += [sums_ref[line : line + 1, k * 128 : (k + 1) * 128] for k in range(3)]
        pieces.append(jnp.zeros((3, 128), FLOAT))
        message_ref[pl.ds(pl.multiple_of(first_half + AT_SUMS, 8), 24), :] = jnp.concatenate(
            pieces, axis=0
        )


def feed_forward(core, attn, pooled, cot, w_short, w_out, gain, shift, w1, b1, w2, b2):
    row_block = lambda width: pl.BlockSpec((FC_ROWS, width), lambda i: (i, 0))
    lane_block = lambda groups: pl.BlockSpec((groups, FC_ROWS, 128), lambda i: (0, i, 0))
    return pl.pallas_call(
        feed_kernel,
        grid=(FC_STEPS,),
        in_specs=[
            pl.BlockSpec(memory_space=pltpu.SMEM),
            lane_block(3),
            lane_block(2),
            row_block(D),
            whole((D_IN, D)),
            whole((D, D)),
            whole((1, D)),
            whole((1, D)),
            whole((D, FF)),
            whole((1, FF)),
            whole((FF, D)),
            whole((1, D)),
        ],
        out_specs=[
            row_block(D),
            whole((3, ROWS_P, 128)),
            whole((2, ROWS_P, 128)),
            whole((2 * HALF_ROWS, 128)),
        ],
        out_shape=[
            jax.ShapeDtypeStruct((ROWS, D), FLOAT),
            jax.ShapeDtypeStruct((3, ROWS_P, 128), FLOAT),
            jax.ShapeDtypeStruct((2, ROWS_P, 128), FLOAT),
            jax.ShapeDtypeStruct((2 * HALF_ROWS, 128), FLOAT),
        ],
        scratch_shapes=[pltpu.VMEM((1, FF), FLOAT), pltpu.VMEM((8, D), FLOAT)],
        compiler_params=params(),
        name="feed_forward",
        cost_estimate=cost(1.2e10, 2e7, 3e6),
    )(core, attn, pooled, cot, w_short, w_out, gain, shift, w1, b1, w2, b2)


def unpack_kernel(
    core_ref, own_ref, other_ref, g1_ref, g2_ref, gout_ref, gshort_ref, sums1_ref, sums_ref
):
    def first(ref):
        for k in range(FF // 128):
            g1_ref[:, k * 128 : (k + 1) * 128] = ref[k * D : (k + 1) * D, :]
        for k in range(2):
            at = AT_OUT0 + k * D
            gout_ref[:, k * 128 : (k + 1) * 128] = ref[at : at + D, :]
        gshort_ref[:, :128] = ref[AT_SHORT0 : AT_SHORT0 + D_IN, :]
        lines = ref[AT_SUMS : AT_SUMS + 24, :]
        for k in range(FF // 128):
            sums1_ref[:, k * 128 : (k + 1) * 128] = lines[k : k + 1, :]
        sums_ref[...] = jnp.zeros_like(sums_ref)
        for line in range(3):
            for k in range(3):
                at = FF // 128 + line * 3 + k
                sums_ref[line : line + 1, k * 128 : (k + 1) * 128] = lines[at : at + 1, :]

    def second(ref):
        for k in range(FF // 128):
            g2_ref[k * 128 : (k + 1) * 128, :] = ref[k * D : (k + 1) * D, :].T
        gout_ref[:, 2 * 128 :] = ref[AT_OUT1 : AT_OUT1 + D, :]
        for k in range(2):
            at = AT_SHORT1 + k * D_IN
            gshort_ref[:, (k + 1) * 128 : (k + 2) * 128] = ref[at : at + D_IN, :]

    @pl.when(core_ref[0] == 0)
    def _():
        first(own_ref)
        second(other_ref)

    @pl.when(core_ref[0] != 0)
    def _():
        first(other_ref)
        second(own_ref)


def unpack(core, own, other):
    shapes = [(D, FF), (FF, D), (D, D), (D_IN, D), (1, FF), (8, D)]
    return pl.pallas_call(
        unpack_kernel,
        in_specs=[
            pl.BlockSpec(memory_space=pltpu.SMEM),
            whole((HALF_ROWS, 128)),
            whole((HALF_ROWS, 128)),
        ],
        out_specs=[whole(shape) for shape in shapes],
        out_shape=[jax.ShapeDtypeStruct(shape, FLOAT) for shape in shapes],
        compiler_params=params(),
        name="unpack",
        cost_estimate=cost(1e6, 1.2e7),
    )(core, own, other)


def back_kernel(
    coef_ref,
    x_ref,
    qkv_ref,
    probs_ref,
    dattn_ref,
    dshort_ref,
    bn_scale_ref,
    bn_bias_ref,
    gain_ref,
    shift_ref,
    w_ref,
    dbias_ref,
    gw_ref,
    sums_ref,
    dcells_ref,
):
    crop = pl.program_id(0)

    @pl.when(crop == 0)
    def _():
        dbias_ref[...] = jnp.zeros_like(dbias_ref)
        gw_ref[...] = jnp.zeros_like(gw_ref)
        sums_ref[...] = jnp.zeros_like(sums_ref)

    dattn = take_rows(dattn_ref, crop).astype(HALF)
    key_t = qkv_ref[0, :, D : 2 * D].astype(FLOAT).T.astype(HALF)
    masks = head_masks()
    dquery_t, dkeys, dvalues = [], [], []
    for group in range(3):
        lanes = slice(group * 128, (group + 1) * 128)
        query_all = qkv_ref[0, :, lanes]
        value = qkv_ref[0, :, 2 * D + group * 128 : 2 * D + (group + 1) * 128]
        dkey = jnp.zeros((TP, 128), FLOAT)
        dvalue = jnp.zeros((TP, 128), FLOAT)
        for k in range(4):
            head = group * 4 + k
            grad = dattn[:, lanes] * masks[k]
            query = query_all * masks[k]
            probs = probs_ref[0, head]
            wide = probs.astype(FLOAT)
            dprobs = dot(value, grad, NT)
            shared = jnp.sum(dprobs * wide, axis=0, keepdims=True)
            dscores = (wide * (dprobs - shared)).astype(HALF)
            dbias_ref[head] += dscores.astype(FLOAT)
            dvalue = dvalue + dot(probs, grad)
            dkey = dkey + dot(dscores, query)
            dquery_t.append(dot(key_t[head * HEAD : (head + 1) * HEAD, :], dscores))
        dkeys.append(dkey)
        dvalues.append(dvalue)
    dquery = jnp.concatenate(dquery_t, axis=0).T
    dqkv = jnp.concatenate(
        [dquery * SCALE] + [dkey * SCALE for dkey in dkeys] + dvalues, axis=1
    ).astype(HALF)
    parts = pool_parts(x_ref, coef_ref[0:1, :], coef_ref[1:2, :], bn_scale_ref[...], bn_bias_ref[...])
    top = jnp.maximum(jnp.maximum(parts[0], parts[1]), jnp.maximum(parts[2], parts[3]))
    pooled = top + jnp.log(sum(jnp.exp(part - top) for part in parts))
    z, inverse = norm_rows(pooled)
    first_t = (z * gain_ref[...] + shift_ref[...]).T.astype(HALF)
    gw_ref[...] += dot(first_t, dqkv)
    dfirst = dot(dqkv, w_ref[...], NT)
    dz = dfirst * gain_ref[...]
    dpooled = take_rows(dshort_ref, crop)[:, :D_IN] + inverse * (
        dz
        - jnp.mean(dz, axis=-1, keepdims=True)
        - z * jnp.mean(dz * z, axis=-1, keepdims=True)
    )
    sums_ref[0:1, :] += jnp.sum(dfirst * z, axis=0, keepdims=True)
    sums_ref[1:2, :] += jnp.sum(dfirst, axis=0, keepdims=True)
    along = jnp.zeros((TP, D_IN), FLOAT)
    total = jnp.zeros((TP, D_IN), FLOAT)
    for part in range(4):
        dpart = dpooled * jnp.exp(parts[part] - pooled)
        dcells_ref[0, part * TP : (part + 1) * TP, :] = dpart
        raw = x_ref[0, part * TP : (part + 1) * TP, :].astype(FLOAT)
        along = along + dpart * (raw - coef_ref[0:1, :])
        total = total + dpart
    sums_ref[2:3, :] += jnp.sum(along, axis=0, keepdims=True) * coef_ref[1:2, :]
    sums_ref[3:4, :] += jnp.sum(total, axis=0, keepdims=True)


def attention_back(coef, picked, qkv, probs, dattn, dshort, bn_scale, bn_bias, gain, shift, w_qkv):
    return pl.pallas_call(
        back_kernel,
        grid=(CROPS,),
        in_specs=[
            whole((8, D_IN)),
            pl.BlockSpec((1, 4 * TP, D_IN), lambda c: (c, 0, 0)),
            pl.BlockSpec((1, TP, 3 * D), lambda c: (c, 0, 0)),
            pl.BlockSpec((1, HEADS, TP, TP), lambda c: (c, 0, 0, 0)),
            whole((3, ROWS_P, 128)),
            whole((2, ROWS_P, 128)),
            whole((1, D_IN)),
            whole((1, D_IN)),
            whole((1, D_IN)),
            whole((1, D_IN)),
            whole((D_IN, 3 * D)),
        ],
        out_specs=[
            whole((HEADS, TP, TP)),
            whole((D_IN, 3 * D)),
            whole((8, D_IN)),
            pl.BlockSpec((1, 4 * TP, D_IN), lambda c: (c, 0, 0)),
        ],
        out_shape=[
            jax.ShapeDtypeStruct((HEADS, TP, TP), FLOAT),
            jax.ShapeDtypeStruct((D_IN, 3 * D), FLOAT),
            jax.ShapeDtypeStruct((8, D_IN), FLOAT),
            jax.ShapeDtypeStruct((CROPS, 4 * TP, D_IN), FLOAT),
        ],
        compiler_params=params(),
        name="attention_back",
        cost_estimate=cost(6e9, 4e7, 2e6),
    )(coef, picked, qkv, probs, dattn, dshort, bn_scale, bn_bias, gain, shift, w_qkv)


def scatter_kernel(s_ref, d_ref, out_ref):
    value = d_ref[0]
    hi = value.astype(HALF)
    lo = (value - hi.astype(FLOAT)).astype(HALF)
    out_ref[0] = dot(hi, s_ref[...], TN) + dot(lo, s_ref[...], TN)


def scatter_cells(picks, dcells):
    return pl.pallas_call(
        scatter_kernel,
        grid=(CROPS,),
        in_specs=[
            whole((4 * TP, CELLS)),
            pl.BlockSpec((1, 4 * TP, D_IN), lambda c: (c, 0, 0)),
        ],
        out_specs=pl.BlockSpec((1, D_IN, CELLS), lambda c: (c, 0, 0)),
        out_shape=jax.ShapeDtypeStruct((CROPS, D_IN, CELLS), FLOAT),
        compiler_params=params(),
        name="scatter_cells",
        cost_estimate=cost(6e9, 1.2e7),
    )(picks, dcells)


def column(row):
    return jnp.broadcast_to(row, (128, D_IN)).T[:, 0:1]


def cells_kernel(gathered_ref, coef_ref, scale_ref, d_ref, x_ref, out_ref, sums_ref, cols_ref):
    @pl.when(pl.program_id(0) == 0)
    def _():
        gathered = gathered_ref[...]
        total = jnp.sum(gathered, axis=0)
        along = total[:, 0:D_IN]
        plain = total[:, 256 : 256 + D_IN]
        sums_ref[...] = jnp.zeros_like(sums_ref)
        sums_ref[0:1, :] = along
        sums_ref[1:2, :] = plain
        mean = coef_ref[0:1, :]
        inv = coef_ref[1:2, :]
        factor = inv * scale_ref[...]
        count = 1.0 / float(gathered.shape[0] * CROPS * CELLS)
        slope = factor * along * inv * count
        cols_ref[:, 0:1] = column(factor)
        cols_ref[:, 1:2] = column(factor * plain * count)
        cols_ref[:, 2:3] = column(slope)
        cols_ref[:, 3:4] = column(mean)

    out_ref[0] = (
        d_ref[0] * cols_ref[:, 0:1]
        - cols_ref[:, 1:2]
        - (x_ref[0].astype(FLOAT) - cols_ref[:, 3:4]) * cols_ref[:, 2:3]
    )


def cell_gradient(gathered, coef, bn_scale, dcells, cells):
    crop_block = pl.BlockSpec((1, D_IN, CELLS), lambda c: (c, 0, 0))
    return pl.pallas_call(
        cells_kernel,
        grid=(CROPS,),
        in_specs=[
            whole(gathered.shape),
            whole((8, D_IN)),
            whole((1, D_IN)),
            crop_block,
            crop_block,
        ],
        out_specs=[crop_block, whole((8, D_IN))],
        out_shape=[
            jax.ShapeDtypeStruct((CROPS, D_IN, CELLS), FLOAT),
            jax.ShapeDtypeStruct((8, D_IN), FLOAT),
        ],
        scratch_shapes=[pltpu.VMEM((D_IN, 128), FLOAT)],
        compiler_params=params(),
        name="cell_gradient",
        cost_estimate=cost(1e7, 1.5e7),
    )(gathered, coef, bn_scale, dcells, cells)


CHIPS = ("y", "x", "z")
ALL = ("y", "x", "z", "core")


def gather_rows(copies):
    if copies.shape[0] == 1:
        return copies
    return lax.all_to_all(copies, ALL, 0, 0)


def sum_early(message, count):
    if count == 1:
        return message[0], message[1]
    swap = [(0, 1), (1, 0)]
    mine = message[0] + lax.ppermute(message[1], "core", swap)
    pieces = lax.all_to_all(mine.reshape(PIECES, -1, 128), CHIPS, 0, 0)
    piece = jnp.sum(pieces, axis=0)
    copies = jnp.broadcast_to(piece[None], pieces.shape)
    own = lax.all_to_all(copies, CHIPS, 0, 0).reshape(HALF_ROWS, 128)
    return own, lax.ppermute(own, "core", swap)


def sum_late(message, count):
    if count == 1:
        return message
    pieces = lax.all_to_all(message.reshape(count, -1, 128), ALL, 0, 0)
    copies = jnp.broadcast_to(jnp.sum(pieces, axis=0)[None], pieces.shape)
    return lax.all_to_all(copies, ALL, 0, 0).reshape(LATE_ROWS, 128)


def on_device(
    count,
    features,
    bn_scale,
    bn_bias,
    w_short,
    ln1_gain,
    ln1_bias,
    w_qkv,
    rel_table,
    w_out,
    ln2_gain,
    ln2_bias,
    w_fc1,
    fc1_bias,
    w_fc2,
    fc2_bias,
    cotangent,
):
    row = lambda v: v.reshape(1, -1)
    picks = jnp.asarray(select_matrix(), HALF)
    spread = jnp.asarray(spread_matrix(), HALF)
    spread_back = jnp.asarray(reverse_spread_matrix(), HALF)
    core = lax.axis_index("core").astype(jnp.int32).reshape(1)
    cells = features.transpose(0, 2, 1)
    cot = cotangent.transpose(1, 0, 2).reshape(ROWS, D)
    stats = gather_rows(local_stats(cells, count))
    picked = select_cells(picks, cells)
    bias = expand_bias(rel_table, spread)
    qkv, probs, attn, pooled, coef = attention(
        stats, picked, row(bn_scale), row(bn_bias), row(ln1_gain), row(ln1_bias), w_qkv, bias
    )
    out, dattn, dshort, message = feed_forward(
        core,
        attn,
        pooled,
        cot,
        w_short,
        w_out,
        row(ln2_gain),
        row(ln2_bias),
        w_fc1,
        row(fc1_bias),
        w_fc2,
        row(fc2_bias),
    )
    own, other = sum_early(message.reshape(2, HALF_ROWS, 128), count)
    dbias, gqkv, sums, dcells = attention_back(
        coef,
        picked,
        qkv,
        probs,
        dattn,
        dshort,
        row(bn_scale),
        row(bn_bias),
        row(ln1_gain),
        row(ln1_bias),
        w_qkv,
    )
    bn_message = jnp.pad(sums[2:4], ((0, 0), (0, 256 - D_IN))).reshape(1, 1, 512)
    gathered = gather_rows(jnp.broadcast_to(bn_message, (count, 1, 512)))
    scattered = scatter_cells(picks, dcells)
    table = reduce_table(dbias, spread_back)
    late = jnp.concatenate(
        [gqkv[:, k * 128 : (k + 1) * 128] for k in range(9)]
        + [
            table.reshape(HEADS * 6, 128),
            jnp.pad(sums[0:2], ((0, 0), (0, 256 - D_IN))).reshape(4, 128),
        ],
        axis=0,
    )
    late = sum_late(jnp.pad(late, ((0, LATE_ROWS - late.shape[0]), (0, 0))), count)
    grad_cells, bn_sums = cell_gradient(gathered, coef, row(bn_scale), scattered, cells)
    g1, g2, gout, gshort, sums1, sums2 = unpack(core, own, other)
    gqkv = jnp.concatenate([late[k * D_IN : (k + 1) * D_IN] for k in range(9)], axis=1)
    at = 9 * D_IN
    grad_table = late[at : at + HEADS * 6].reshape(HEADS, TAB)[:, : REL * REL][:, ::-1]
    sums = late[at + HEADS * 6 : at + HEADS * 6 + 4].reshape(2, 256)[:, :D_IN]
    return (
        out.reshape(TOK, CROPS, D).transpose(1, 0, 2),
        grad_cells.transpose(0, 2, 1),
        bn_sums[0],
        bn_sums[1],
        gshort,
        sums[0],
        sums[1],
        gqkv,
        grad_table,
        gout,
        sums2[0],
        sums2[1],
        g1,
        sums1[0],
        g2,
        sums2[2],
    )


def solution(mesh):
    count = mesh.size
    shape = (4, 4, 4, 2) if count == 128 else (1, 1, 1, 1)
    grid = jax.sharding.Mesh(mesh.devices.reshape(shape), ALL)
    split = P(ALL, None, None)
    same = P()
    in_specs = (split,) + (same,) * 14 + (split,)
    out_specs = (split, split) + (same,) * 14

    def run(*args):
        return on_device(count, *args)

    return jax.shard_map(run, mesh=grid, in_specs=in_specs, out_specs=out_specs, check_vma=False)
```

time: 589 us -> 314 us (0.53)
  Pallas kernels: 0 us -> 166 us
  blocking collectives: 197 us -> 48.8 us
  matrix products: 138 us -> 0 us
  local copies, waits for them, and re-layouts: 141 us -> 20.5 us
  other arithmetic: 93.3 us -> 4.95 us
  starting transfers between devices: 0.04 us -> 37.3 us
  waiting for transfers between devices: 0.02 us -> 33.6 us
  between operations: 15 us -> 0.98 us
    psum x3 -> x0, blocking collectives: 197 us -> none  [the longest x1 68.2 us: on_device(): sum_rows = lax.psum(jnp.sum(values_in, axis=(0, 1)), 'dp')]
    pallas_call x0 -> x10, Pallas kernels: none -> 166 us  [the longest x1 38.5 us: feed_forward(): pl.pallas_call(feed_kernel, grid=(FC_STEPS,), in_specs=[pl.BlockSpec(memo...]
    dot_general x25 -> x0, matrix products: 138 us -> none  [the longest x1 18.3 us: on_device(): jnp.einsum('cihd,cjhd->chij', mixed_grad, value_part, preferred_element_t...]
    all_to_all x0 -> x1, blocking collectives: none -> 48.8 us  [sum_early(): pieces = lax.all_to_all(mine.reshape(PIECES, -1, 128), CHIPS, 0, 0)]
    reshape x7 -> x8, local copies, waits for them, and re-layouts: 49.6 us -> 2.97 us  [the longest x4 2.29 us: on_device(): row = lambda v: v.reshape(1, -1)]
    reduce_sum x12 -> x2, other arithmetic: 47.6 us -> 3.35 us  [the longest x1 1.98 us: sum_early(): piece = jnp.sum(pieces, axis=0)]
    add x5 -> x0, local copies, waits for them, and re-layouts: 43.1 us -> none  [the longest x2 40 us: on_device(): jnp.einsum('cihd,cjhd->chij', query, key_part, preferred_element_type=FLOAT)]
    all_to_all x0 -> x5, starting transfers between devices: none -> 37.1 us  [the longest x2 15.8 us: gather_rows(): return lax.all_to_all(copies, ALL, 0, 0)]
  transfers between devices with their start and end apart: 1 -> 7, of which waited for: 0 -> 3; matrix products, arithmetic and copies ran while one was open for 16% -> 5% of each run, Pallas kernels for 0% -> 28%
where the time goes in v1:
time: 314 us; the launch traced here: 312 us
  Pallas kernels  166 us (53%)
  blocking collectives  48.8 us (16%)
  starting transfers between devices  37.3 us (12%)
  waiting for transfers between devices  33.6 us (11%)
  local copies, waits for them, and re-layouts  20.5 us (7%)
  other arithmetic  4.95 us (2%)
    all_to_all x1, blocking collectives, sum_early(): pieces = lax.all_to_all(mine.reshape(PIECES, -1, 128), CHIPS, 0, 0)  48.8 us
    pallas_call x1, Pallas kernels, feed_forward(): pl.pallas_call(feed_kernel, grid=(FC_STEPS,), in_specs=[pl.BlockSpec(memo...  38.5 us
    pallas_call x1, Pallas kernels, attention_back(): pl.pallas_call(back_kernel, grid=(CROPS,), in_specs=[whole((8, D_IN)), pl...  37.9 us
    pallas_call x1, Pallas kernels, attention(): pl.pallas_call(attention_kernel, grid=(CROPS,), in_specs=[whole(gathered....  29.5 us
    all_to_all x1, waiting for transfers between devices, sum_late(): pieces = lax.all_to_all(message.reshape(count, -1, 128), ALL, 0, 0)  18.7 us
    all_to_all x2, starting transfers between devices, gather_rows(): return lax.all_to_all(copies, ALL, 0, 0)  15.8 us
    pallas_call x1, Pallas kernels, scatter_cells(): pl.pallas_call(scatter_kernel, grid=(CROPS,), in_specs=[whole((4 * TP, CE...  12 us
    all_to_all x1, starting transfers between devices, sum_late(): pieces = lax.all_to_all(message.reshape(count, -1, 128), ALL, 0, 0)  10.5 us
  transfers between devices with their start and end apart: 7, of which 3 were waited for; matrix products, arithmetic and copies ran while one was open for 5% of the time, Pallas kernels for 28%

profile of v1, /device:TPU:0, one launch (start us, length us, event | category | flops | bytes accessed | tf_op | source)
XLA Modules:
  0.0 311.7 jit_solution(13132189413519008629)
XLA Ops:
  0.6 0.0 copy-start.8
  0.7 0.0 copy-start.9
  0.7 0.0 copy-start.10
  0.7 0.0 copy-start.7
  0.7 0.0 copy-start.5
  0.7 3.9 %stats.1 = f32[128,1,512]{2,1,0:T(1,128)} custom-call(bf16[8,192,784]{2,1,0:T(8,128)(2,1)} %bitcast.39), custom_call_target="tpu_custom_call" | custom-call | flops 8000000 | bytes 2800000 | tf_op jit(solution)/shard_map/stats/pallas_call | solution.py:113
  4.6 11.1 %all-to-all-start = ((f32[128,1,512]{2,1,0:T(1,128)}), f32[128,1,512]{2,1,0:T(1,128)S(1)}, u32[]{:S(2)}, u32[]{:S(2)}) async-start(f32[128,1,512]{2,1,0:T(1,128)} %stats.1), calls=%async_computation | async-start | bytes 524288 | tf_op jit(solution)/shard_map/all_to_all | solution.py:776
  15.7 0.0 copy-done.8
  15.8 0.6 reshape.124.gain_ref
  16.3 0.0 copy-done.9
  16.3 0.6 reshape.125.shift_ref
  16.9 0.0 copy-done.10
  16.9 0.6 reshape.127.b2_ref
  17.5 0.0 copy-done.7
  17.5 0.6 reshape.126.b1_ref
  18.1 0.0 copy-done.5
  18.1 0.6 reshape.122.table_ref
  18.7 9.1 %expand_bias.1.bias_ref = f32[12,208,208]{2,1,0:T(8,128)} custom-call(f32[12,1,768]{2,1,0:T(1,128)} %reshape.122.table_ref, bf16[384,208]{1,0:T(8,128)(2,1)} %constant.15.clone.spread_ref), custom_call_target="tpu_custom_call" | custom-call | flops 2000000000 | bytes 3000000 | tf_op jit(solution)/shard_map/expand_bias/pallas_call | solution.py:171
  27.8 8.9 %select_cells.1.x_ref = bf16[8,832,192]{2,1,0:T(8,128)(2,1)} custom-call(bf16[832,784]{1,0:T(8,128)(2,1)} %constant.14.clone.s_ref, bf16[8,192,784]{2,1,0:T(8,128)(2,1)} %bitcast.40), custom_call_target="tpu_custom_call" | custom-call | flops 3000000000 | bytes 7000000 | tf_op jit(solution)/shard_map/select_cells/pallas_call | solution.py:140
  36.7 0.0 all-to-all-done.gathered_ref
  36.7 0.7 copy-done.4
  37.4 29.5 %attention.1 = (bf16[8,208,1152]{2,1,0:T(8,128)(2,1)}, bf16[8,12,208,208]{3,2,1,0:T(8,128)(2,1)}, f32[3,1664,128]{2,1,0:T(8,128)}, f32[2,1664,128]{2,1,0:T(8,128)}, f32[8,192]{1,0:T(8,128)}) custom-call(f32[128,1,512]{2,1,0:T(1,128)} %copy-done.4, bf16[8,832,192]{2,1,0:T(8,128)(2,1)} %select_cells.1.x_ref, f32[1,192]{1,0:T(1,128)} %bitcast.58, ...), custom_call_target="tpu_custom_call" | custom-call | flops 4000000000 | bytes 25000000 | tf_op jit(solution)/shard_map/attention/pallas_call | solution.py:307
  67.0 38.5 %feed_forward.1 = (f32[1568,384]{1,0:T(8,128)}, f32[3,1664,128]{2,1,0:T(8,128)}, f32[2,1664,128]{2,1,0:T(8,128)}, f32[11264,128]{1,0:T(8,128)}) custom-call(s32[1]{0:T(128)} %bitcast.core_ref, f32[3,1664,128]{2,1,0:T(8,128)} %get-tuple-element.37.attn_ref, f32[2,1664,128]{2,1,0:T(8,128)} %get-tuple-element.38.pooled_ref, bf16[1568,384]{1,0:T(8,128)(2,1)} %bitcast.62, ...), custom_call_target="tpu_custom_call" | custom-call | flops 12000000000 | bytes 20000000 | tf_op jit(solution)/shard_map/feed_forward/pallas_call | solution.py:484
  105.5 2.2 slice.132
  107.7 0.1 collective-permute-start
  107.8 5.3 %collective-permute-done = f32[5632,128]{1,0:T(8,128)S(1)} collective-permute-done((f32[5632,128]{1,0:T(8,128)S(1)}, f32[5632,128]{1,0:T(8,128)S(1)}, u32[]{:S(2)}, u32[]{:S(2)}) %collective-permute-start) | collective-permute-done | bytes 2883616 | tf_op jit(solution)/shard_map/ppermute | solution.py:783
  113.0 0.3 slice_add_fusion
  113.3 48.8 %all_to_all.30 = f32[64,88,128]{2,1,0:T(8,128)} all-to-all(f32[64,88,128]{2,1,0:T(8,128)S(1)} %bitcast.38), channel_id=1, replica_groups=mesh['y'=4,'x'=4,'z'=4,'core'=2] {'y','x','z'}, dimensions={0} | all-to-all | bytes 5767168 | tf_op jit(solution)/shard_map/all_to_all | solution.py:784
  162.1 2.0 reduce_sum.18
  164.1 1.8 broadcast_in_dim.10
  165.9 5.1 %all-to-all-start.3 = ((f32[64,88,128]{2,1,0:T(8,128)}), f32[64,88,128]{2,1,0:T(8,128)S(1)}, u32[]{:S(2)}, u32[]{:S(2)}) async-start(f32[64,88,128]{2,1,0:T(8,128)} %broadcast_in_dim.10), calls=%async_computation.3 | async-start | bytes 5767168 | tf_op jit(solution)/shard_map/all_to_all | solution.py:787
  171.0 37.9 %attention_back.1 = (f32[12,208,208]{2,1,0:T(8,128)}, f32[192,1152]{1,0:T(8,128)}, f32[8,192]{1,0:T(8,128)}, f32[8,832,192]{2,1,0:T(8,128)}) custom-call(f32[8,192]{1,0:T(8,128)} %get-tuple-element.40.coef_ref, bf16[8,832,192]{2,1,0:T(8,128)(2,1)} %select_cells.1.x_ref, bf16[8,208,1152]{2,1,0:T(8,128)(2,1)} %get-tuple-element.41.qkv_ref, ...), custom_call_target="tpu_custom_call" | custom-call | flops 6000000000 | bytes 40000000 | tf_op jit(solution)/shard_map/attention_back/pallas_call | solution.py:657
  208.9 0.8 fusion.1
  209.8 10.4 %reduce_table.1 = f32[12,1,768]{2,1,0:T(1,128)} custom-call(f32[12,208,208]{2,1,0:T(8,128)} %get-tuple-element.52.d_ref, bf16[208,384]{1,0:T(8,128)(2,1)} %constant.16.clone.spread_ref), custom_call_target="tpu_custom_call" | custom-call | flops 2000000000 | bytes 3000000 | tf_op jit(solution)/shard_map/reduce_table/pallas_call | solution.py:202
  220.1 0.0 copy-done.3
  220.3 0.8 constant_dynamic-update-slice_fusion.1
  221.1 1.0 pad.18
  222.1 0.0 all-to-all-done.3
  222.1 10.5 %all-to-all-start.4 = ((f32[128,16,128]{2,1,0:T(8,128)}), f32[128,16,128]{2,1,0:T(8,128)}, u32[]{:S(2)}, u32[]{:S(2)}) async-start(f32[128,16,128]{2,1,0:T(8,128)} %bitcast.42), calls=%async_computation.4 | async-start | bytes 2097152 | tf_op jit(solution)/shard_map/all_to_all | solution.py:794
  232.6 0.1 collective-permute-start.1
  232.8 18.7 %all-to-all-done.4 = f32[128,16,128]{2,1,0:T(8,128)} async-done(((f32[128,16,128]{2,1,0:T(8,128)}), f32[128,16,128]{2,1,0:T(8,128)}, u32[]{:S(2)}, u32[]{:S(2)}) %all-to-all-start.4) | async-done | bytes 1048608 | tf_op jit(solution)/shard_map/all_to_all | solution.py:794
  251.5 0.8 broadcast_in_dim.9
  252.3 4.6 %all-to-all-start.1 = ((f32[128,1,512]{2,1,0:T(1,128)}), f32[128,1,512]{2,1,0:T(1,128)S(1)}, u32[]{:S(2)}, u32[]{:S(2)}) async-start(f32[128,1,512]{2,1,0:T(1,128)} %broadcast_in_dim.9), calls=%async_computation.1 | async-start | bytes 524288 | tf_op jit(solution)/shard_map/all_to_all | solution.py:776
  257.0 1.4 reduce_sum.19
  258.3 9.6 %all-to-all-done.1.gathered_ref = f32[128,1,512]{2,1,0:T(1,128)S(1)} async-done(((f32[128,1,512]{2,1,0:T(1,128)}), f32[128,1,512]{2,1,0:T(1,128)S(1)}, u32[]{:S(2)}, u32[]{:S(2)}) %all-to-all-start.1) | async-done | bytes 262176 | tf_op jit(solution)/shard_map/all_to_all | solution.py:776
  267.9 1.1 broadcast_in_dim.22
  268.9 5.8 %all-to-all-start.5 = ((f32[128,16,128]{2,1,0:T(8,128)}), f32[128,16,128]{2,1,0:T(8,128)}, u32[]{:S(2)}, u32[]{:S(2)}) async-start(f32[128,16,128]{2,1,0:T(8,128)} %broadcast_in_dim.22), calls=%async_computation.5 | async-start | bytes 2097152 | tf_op jit(solution)/shard_map/all_to_all | solution.py:796
  274.7 12.0 %scatter_cells.1.d_ref = f32[8,192,784]{2,1,0:T(8,128)} custom-call(bf16[832,784]{1,0:T(8,128)(2,1)} %constant.14.clone.s_ref, f32[8,832,192]{2,1,0:T(8,128)} %get-tuple-element.46.d_ref), custom_call_target="tpu_custom_call" | custom-call | flops 6000000000 | bytes 12000000 | tf_op jit(solution)/shard_map/scatter_cells/pallas_call | solution.py:699
  286.7 0.0 copy-done.2
  286.7 9.2 %cell_gradient.1 = (f32[8,192,784]{2,1,0:T(8,128)}, f32[8,192]{1,0:T(8,128)}) custom-call(f32[128,1,512]{2,1,0:T(1,128)} %copy-done.2, f32[8,192]{1,0:T(8,128)} %get-tuple-element.40.coef_ref, f32[1,192]{1,0:T(1,128)} %bitcast.60, f32[8,192,784]{2,1,0:T(8,128)} %scatter_cells.1.d_ref, bf16[8,192,784]{2,1,0:T(8,128)(2,1)} %bitcast.41), custom_call_target="tpu_custom_call" | custom-call | flops 10000000 | bytes 15000000 | tf_op jit(solution)/shard_map/cell_gradient/pallas_call | solution.py:747
  296.0 1.3 fusion.2
  297.3 0.0 all-to-all-done.5
  297.3 0.7 slice.169
  298.0 0.8 slice.181
  298.8 0.4 reverse
  299.2 0.7 slice.196
  299.9 1.3 fusion
  301.4 0.0 copy-start.6
  301.4 0.9 copy-done.6
  302.3 0.6 fusion.3
  302.9 0.0 collective-permute-done.1.other_ref
  302.9 6.1 %unpack.1 = (f32[384,1536]{1,0:T(8,128)}, f32[1536,384]{1,0:T(8,128)}, f32[384,384]{1,0:T(8,128)}, f32[192,384]{1,0:T(8,128)}, f32[1,1536]{1,0:T(1,128)}, /*index=5*/f32[8,384]{1,0:T(8,128)}) custom-call(s32[1]{0:T(128)} %bitcast.core_ref, f32[5632,128]{1,0:T(8,128)} %bitcast.37, f32[5632,128]{1,0:T(8,128)} %collective-permute-done.1.other_ref), custom_call_target="tpu_custom_call" | custom-call | flops 1000000 | bytes 12000000 | tf_op jit(solution)/shard_map/unpack/pallas_call | solution.py:560
  309.0 1.4 slice_reduce_fusion
  310.4 1.3 reduce.2
  (33 shorter events, 0.2 us)
Async XLA Ops:
  0.6 15.1 %copy-start.8 = (f32[384]{0:T(512)S(1)}, f32[384]{0:T(512)}, u32[]{:S(2)}) copy-start(f32[384]{0:T(512)} %param.28) | copy-start | bytes 4612
  0.7 15.7 %copy-start.9 = (f32[384]{0:T(512)S(1)}, f32[384]{0:T(512)}, u32[]{:S(2)}) copy-start(f32[384]{0:T(512)} %param.29) | copy-start | bytes 4612
  0.7 16.2 %copy-start.10 = (f32[384]{0:T(512)S(1)}, f32[384]{0:T(512)}, u32[]{:S(2)}) copy-start(f32[384]{0:T(512)} %param.33) | copy-start | bytes 4612
  0.7 16.8 %copy-start.7 = (f32[1536]{0:T(1024)S(1)}, f32[1536]{0:T(1024)}, u32[]{:S(2)}) copy-start(f32[1536]{0:T(1024)} %param.31) | copy-start | bytes 18436
  0.7 17.4 %copy-start.5 = (f32[12,729]{1,0:T(8,128)S(1)}, f32[12,729]{1,0:T(8,128)}, u32[]{:S(2)}) copy-start(f32[12,729]{1,0:T(8,128)} %param.26) | copy-start | bytes 104980
  4.6 32.1 %all-to-all-start = ((f32[128,1,512]{2,1,0:T(1,128)}), f32[128,1,512]{2,1,0:T(1,128)S(1)}, u32[]{:S(2)}, u32[]{:S(2)}) async-start(f32[128,1,512]{2,1,0:T(1,128)} %stats.1), calls=%async_computation | async-start | bytes 524288 | tf_op jit(solution)/shard_map/all_to_all | solution.py:776
  36.7 0.7 copy-start.4
  105.5 7.5 %copy-start.1 = (f32[11264,128]{1,0:T(8,128)S(1)}, f32[11264,128]{1,0:T(8,128)}, u32[]{:S(2)}) copy-start(f32[11264,128]{1,0:T(8,128)} %get-tuple-element.49) | copy-start | bytes 17301508
  107.7 5.4 %collective-permute-start = (f32[5632,128]{1,0:T(8,128)S(1)}, f32[5632,128]{1,0:T(8,128)S(1)}, u32[]{:S(2)}, u32[]{:S(2)}) collective-permute-start(f32[5632,128]{1,0:T(8,128)S(1)} %slice.132), channel_id=1, source_target_pairs={{0,1},{1,0},{2,3},{3,2},{4,5},{5,4},{6,7},{7,6},{8,9},{9,8},{10,11... | collective-permute-start | bytes 8650760 | tf_op jit(solution)/shard_map/ppermute | solution.py:783
  165.9 56.2 %all-to-all-start.3 = ((f32[64,88,128]{2,1,0:T(8,128)}), f32[64,88,128]{2,1,0:T(8,128)S(1)}, u32[]{:S(2)}, u32[]{:S(2)}) async-start(f32[64,88,128]{2,1,0:T(8,128)} %broadcast_in_dim.10), calls=%async_computation.3 | async-start | bytes 5767168 | tf_op jit(solution)/shard_map/all_to_all | solution.py:787
  209.7 10.4 %copy-start.3 = (f32[192,1152]{1,0:T(8,128)S(1)}, f32[192,1152]{1,0:T(8,128)}, u32[]{:S(2)}) copy-start(f32[192,1152]{1,0:T(8,128)} %get-tuple-element.51) | copy-start | bytes 2654212
  222.1 46.8 %copy-start = (f32[64,88,128]{2,1,0:T(8,128)}, f32[64,88,128]{2,1,0:T(8,128)S(1)}, u32[]{:S(2)}) copy-start(f32[64,88,128]{2,1,0:T(8,128)S(1)} %all-to-all-done.3) | copy-start | bytes 8650756
  222.1 29.4 %all-to-all-start.4 = ((f32[128,16,128]{2,1,0:T(8,128)}), f32[128,16,128]{2,1,0:T(8,128)}, u32[]{:S(2)}, u32[]{:S(2)}) async-start(f32[128,16,128]{2,1,0:T(8,128)} %bitcast.42), calls=%async_computation.4 | async-start | bytes 2097152 | tf_op jit(solution)/shard_map/all_to_all | solution.py:794
  232.6 70.2 %collective-permute-start.1 = (f32[5632,128]{1,0:T(8,128)S(1)}, f32[5632,128]{1,0:T(8,128)}, u32[]{:S(2)}, u32[]{:S(2)}) collective-permute-start(f32[5632,128]{1,0:T(8,128)S(1)} %bitcast.36), channel_id=1, source_target_pairs={{0,1},{1,0},{2,3},{3,2},{4,5},{5,4},{6,7},{7,6},{8,9},{9,8},{10,11... | collective-permute-start | bytes 8650760 | tf_op jit(solution)/shard_map/ppermute | solution.py:788
  252.3 15.6 %all-to-all-start.1 = ((f32[128,1,512]{2,1,0:T(1,128)}), f32[128,1,512]{2,1,0:T(1,128)S(1)}, u32[]{:S(2)}, u32[]{:S(2)}) async-start(f32[128,1,512]{2,1,0:T(1,128)} %broadcast_in_dim.9), calls=%async_computation.1 | async-start | bytes 524288 | tf_op jit(solution)/shard_map/all_to_all | solution.py:776
  267.9 18.8 %copy-start.2 = (f32[128,1,512]{2,1,0:T(1,128)}, f32[128,1,512]{2,1,0:T(1,128)S(1)}, u32[]{:S(2)}) copy-start(f32[128,1,512]{2,1,0:T(1,128)S(1)} %all-to-all-done.1.gathered_ref) | copy-start | bytes 786436
  268.9 28.4 %all-to-all-start.5 = ((f32[128,16,128]{2,1,0:T(8,128)}), f32[128,16,128]{2,1,0:T(8,128)}, u32[]{:S(2)}, u32[]{:S(2)}) async-start(f32[128,16,128]{2,1,0:T(8,128)} %broadcast_in_dim.22), calls=%async_computation.5 | async-start | bytes 2097152 | tf_op jit(solution)/shard_map/all_to_all | solution.py:796
  301.4 0.9 copy-start.6
